TPU v7x, 32 devices: a whole 2x2x4 slice. The times are simulated.
32 devices in a mesh: group: 2 (over x), ep: 16 (over z, y, core).
Axes of the slice: x: 2, y: 2, z: 4, core: 2. Of those that a mesh axis runs over, the one named last changes fastest.
Arguments:
- tokens: bfloat16 [4096, 4096], P(('group', 'ep')), parts along dimension 0, may hold values from -6 to 6
- expert_ids: int32 [4096, 8], P(('group', 'ep')), parts along dimension 0, may hold values from 0 to 15, all different within a row; in each aligned block of 128 rows (0 to 127, 128 to 255, ...) at most 80 rows name the same one
- route_weights: bfloat16 [4096, 8], P(('group', 'ep')), parts along dimension 0, may hold values from 0.049804688 to 1
- smooth: float32 [4096], replicated, may hold values from 0.3 to 3
- gate_weight: bfloat16 [16, 4096, 768], P('ep'), may hold values from -0.09375 to 0.09375
- up_weight: bfloat16 [16, 4096, 768], P('ep'), may hold values from -0.09375 to 0.09375
- down_weight: bfloat16 [16, 768, 4096], P('ep'), may hold values from -0.21875 to 0.21875
Outputs:
- mixed: bfloat16 [4096, 4096], P(('group', 'ep')), parts along dimension 0
There are 2 independent parts, one for each index of `group`. A program takes and returns all parts, laid end to end along the dimension named above; an argument that names none is the same for every part. Nothing has to cross between parts.
Inputs may be any that keep to these rules, and one draw needn't show every extreme that they name: `expert_ids`: A row's 8 ids are distinct. In each aligned block of 128 rows (the rows of one device) no expert is named by more than 80 rows, a bound that some block reaches.
All inputs are finite; a program needn't handle non-finite values.
Results may differ from a plain program's by a relative error of at most 0.007.
Values may be sent and summed in bfloat16 or wider, within the bound.
A program may use at most 128 MiB of HBM per device.

v0:
```python
import jax
import jax.numpy as jnp
from jax import lax
from jax.experimental import pallas as pl
from jax.experimental.pallas import tpu as pltpu
from jax.sharding import PartitionSpec as P

PAD = 128


def ffn_body(a_ref, b_ref, sa_ref, sb_ref, gate_ref, up_ref, down_ref, oa_ref, ob_ref, acc_ref):
    step = pl.program_id(0)
    steps = pl.num_programs(0)
    width = oa_ref.shape[1]
    tile = 512
    for n, (x_ref, s_ref, o_ref) in enumerate(
        ((a_ref, sa_ref, oa_ref), (b_ref, sb_ref, ob_ref))
    ):
        gate = jnp.dot(x_ref[...], gate_ref[...], preferred_element_type=jnp.float32)
        upper = jnp.dot(x_ref[...], up_ref[...], preferred_element_type=jnp.float32)
        hidden = (gate / (1.0 + jnp.exp(-gate)) * upper).astype(jnp.bfloat16)

        for j in range(width // tile):
            cols = pl.ds(j * tile, tile)
            part = jnp.dot(hidden, down_ref[:, cols], preferred_element_type=jnp.float32)

            @pl.when(step == 0)
            def _():
                acc_ref[n, :, cols] = part

            @pl.when((step > 0) & (step < steps - 1))
            def _():
                acc_ref[n, :, cols] += part

            @pl.when(step == steps - 1)
            def _():
                o_ref[:, cols] = ((acc_ref[n, :, cols] + part) * s_ref[...]).astype(o_ref.dtype)


def ffn(a, b, scale_a, scale_b, folded_gate, folded_up, down_one):
    rows = a.shape[0]
    width, hidden = folded_gate.shape
    block = 256
    steps = hidden // block
    whole = lambda i: (0, 0)
    out = jax.ShapeDtypeStruct((rows, width), jnp.bfloat16)
    return pl.pallas_call(
        ffn_body,
        grid=(steps,),
        in_specs=[
            pl.BlockSpec((rows, width), whole),
            pl.BlockSpec((rows, width), whole),
            pl.BlockSpec((rows, 1), whole),
            pl.BlockSpec((rows, 1), whole),
            pl.BlockSpec((width, block), lambda i: (0, i)),
            pl.BlockSpec((width, block), lambda i: (0, i)),
            pl.BlockSpec((block, width), lambda i: (i, 0)),
        ],
        out_specs=[pl.BlockSpec((rows, width), whole)] * 2,
        out_shape=[out, out],
        scratch_shapes=[pltpu.VMEM((2, rows, width), jnp.float32)],
        cost_estimate=pl.CostEstimate(
            flops=12 * rows * width * hidden,
            bytes_accessed=6 * width * hidden + 8 * rows * width,
            transcendentals=2 * rows * hidden,
        ),
        compiler_params=pltpu.CompilerParams(vmem_limit_bytes=48 * 1024 * 1024),
    )(a, b, scale_a, scale_b, folded_gate, folded_up, down_one)


def shards(tokens, expert_ids, route_weights, smooth, gate_weight, up_weight, down_weight):
    tok_dev, topk = expert_ids.shape
    width = tokens.shape[1]
    experts = lax.axis_size("ep")
    me = lax.axis_index("ep")
    chips = experts // 2
    far = chips // 2
    half = tok_dev // 2
    walk = list(range(0, chips, 2)) + list(range(1, chips, 2))[::-1]
    forward = [
        (walk[i] * 2 + c, walk[(i + 1) % chips] * 2 + c) for i in range(chips) for c in range(2)
    ]
    backward = [(b, a) for a, b in forward]
    swap = [(i, i ^ 1) for i in range(experts)]

    def fwd(x):
        return lax.ppermute(x, "ep", forward)

    def bwd(x):
        return lax.ppermute(x, "ep", backward)

    def other(x):
        return lax.ppermute(x, "ep", swap)

    chosen = expert_ids[:, :, None] == jnp.arange(PAD, dtype=jnp.int32)[None, None, :]
    spread = jnp.sum(
        jnp.where(chosen, route_weights[:, :, None].astype(jnp.float32), 0.0), axis=1
    ).astype(jnp.bfloat16)
    own = jnp.concatenate([tokens, spread], axis=1)

    folded_gate = (smooth[:, None] * gate_weight[0].astype(jnp.float32)).astype(jnp.bfloat16)
    folded_up = (smooth[:, None] * up_weight[0].astype(jnp.float32)).astype(jnp.bfloat16)
    down_one = down_weight[0]

    def scale_of(rows):
        mine = jnp.arange(PAD, dtype=jnp.int32)[None, :] == me
        tail = rows[:, width:].astype(jnp.float32)
        return jnp.sum(jnp.where(mine, tail, 0.0), axis=1, keepdims=True)

    def add(*xs):
        total = xs[0].astype(jnp.float32)
        for x in xs[1:]:
            total = total + x.astype(jnp.float32)
        return total.astype(jnp.bfloat16)

    def compute(*blocks):
        mine = jnp.concatenate(blocks, axis=0) if len(blocks) > 1 else blocks[0]
        theirs = other(mine)
        return ffn(
            mine, theirs, scale_of(mine), scale_of(theirs), folded_gate, folded_up, down_one
        )

    behind, ahead = [own], [own]
    parts = [compute(own)]
    for d in range(1, far + 1):
        x, y = behind[-1], ahead[-1]
        if d >= 2:
            x, y, parts[d - 2] = lax.optimization_barrier((x, y, parts[d - 2]))
        if d == far:
            x, y = x[:half], y[half:]
        behind.append(fwd(x))
        ahead.append(bwd(y))
        parts.append(compute(behind[d], ahead[d]))

    sums = [add(p[0], other(p[1])) for p in parts]
    here, last = sums[0], sums[far]
    to_behind = {d: sums[d][:tok_dev] for d in range(1, far)}
    to_ahead = {d: sums[d][tok_dev:] for d in range(1, far)}

    up_sum = fwd(last[:half])
    down_sum = bwd(last[half:])
    for d in range(far - 1, 0, -1):
        if d == far - 1:
            a, b = to_ahead[d], to_behind[d]
            up_sum = jnp.concatenate([add(a[:half], up_sum), a[half:]], axis=0)
            down_sum = jnp.concatenate([b[:half], add(b[half:], down_sum)], axis=0)
        else:
            up_sum = add(to_ahead[d], up_sum)
            down_sum = add(to_behind[d], down_sum)
        up_sum, down_sum = fwd(up_sum), bwd(down_sum)
    return add(here, up_sum, down_sum)


def solution(mesh):
    placed = (
        P(("group", "ep"), None),
        P(("group", "ep"), None),
        P(("group", "ep"), None),
        P(),
        P("ep", None, None),
        P("ep", None, None),
        P("ep", None, None),
    )
    return jax.shard_map(
        shards, mesh=mesh, in_specs=placed, out_specs=P(("group", "ep"), None), check_vma=False
    )
```

profile of v0, /device:TPU:0, one launch (start us, length us, event | category | flops | bytes accessed | tf_op | source)
XLA Modules:
  0.0 314.2 jit_solution(5134370135132186110)
XLA Ops:
  0.0 0.8 copy.26
  0.8 0.8 copy.27
  1.6 0.4 select_reduce_fusion
  1.9 1.3 pad_maximum_fusion.a_ref
  3.2 3.1 collective-permute-start
  6.3 23.9 %collective-permute-done = bf16[128,4224]{1,0:T(8,128)(2,1)} collective-permute-done((bf16[128,4224]{1,0:T(8,128)(2,1)S(1)}, bf16[128,4224]{1,0:T(8,128)(2,1)}, u32[]{:S(2)}, u32[]{:S(2)}) %collective-permute-start) | collective-permute-done | bytes 1081376 | tf_op jit(solution)/shard_map/ppermute | solution.py:87
  30.2 2.3 constant_dynamic-update-slice_fusion.1
  32.5 2.3 constant_dynamic-update-slice_fusion.a_ref
  34.9 11.2 %fusion = (bf16[4096,768]{1,0:T(8,128)(2,1)}, bf16[4096,768]{1,0:T(8,128)(2,1)}) fusion(bf16[1,4096,768]{2,1,0:T(8,128)(2,1)} %param.12, f32[4096]{0:T(1024)S(1)} %copy-done.12, bf16[1,4096,768]{2,1,0:T(8,128)(2,1)} %param.11), kind=kLoop, calls=%fused_computation.1 | loop fusion | flops 18874368 | bytes 25182208 | tf_op jit(solution)/shard_map/convert_element_type | solution.py:102
  46.4 18.9 %shard_map.73 = (bf16[128,4096]{1,0:T(8,128)(2,1)S(1)}, bf16[128,4096]{1,0:T(8,128)(2,1)}) custom-call(bf16[128,4224]{1,0:T(8,128)(2,1)S(1)} %pad_maximum_fusion.a_ref, bf16[128,4224]{1,0:T(8,128)(2,1)S(1)} %collective-permute-done.2.b_ref, f32[128,1]{1,0:T(8,128)S(1)} %copy.28.sa_ref, f32[128,1]{1,0:T(8,128)S(1)} %copy.29.sb_ref, ...), custom_call_target="tpu_custom_call" | custom-call | flops 4831838208 | bytes 23068672 | tf_op jit(solution)/shard_map/pallas_call | solution.py:47
  65.3 1.0 copy-done.6
  66.3 1.8 collective-permute-start.4
  68.1 0.2 collective-permute-start.5
  68.3 1.0 select_reduce_fusion.5
  69.5 0.1 copy.31.sb_ref
  69.6 26.8 %shard_map.74 = (bf16[256,4096]{1,0:T(8,128)(2,1)S(1)}, bf16[256,4096]{1,0:T(8,128)(2,1)}) custom-call(bf16[256,4224]{1,0:T(8,128)(2,1)} %constant_dynamic-update-slice_fusion.a_ref, bf16[256,4224]{1,0:T(8,128)(2,1)} %collective-permute-done.6.b_ref, f32[256,1]{1,0:T(8,128)S(1)} %copy.30.sa_ref, f32[256,1]{1,0:T(8,128)S(1)} %copy.31.sb_ref, ...), custom_call_target="tpu_custom_call" | custom-call | flops 9663676416 | bytes 27262976 | tf_op jit(solution)/shard_map/pallas_call | solution.py:47
  96.4 1.8 collective-permute-start.8
  98.3 1.3 constant_dynamic-update-slice_fusion.3
  99.6 0.5 collective-permute-start.9
  100.3 22.2 %collective-permute-done.8 = bf16[128,4224]{1,0:T(8,128)(2,1)S(1)} collective-permute-done((bf16[128,4224]{1,0:T(8,128)(2,1)}, bf16[128,4224]{1,0:T(8,128)(2,1)S(1)}, u32[]{:S(2)}, u32[]{:S(2)}) %collective-permute-start.8) | collective-permute-done | bytes 1081376 | tf_op jit(solution)/shard_map/ppermute | solution.py:87
  122.5 2.8 collective-permute-done.9
  125.5 4.2 %collective-permute-done.12.b_ref = bf16[256,4224]{1,0:T(8,128)(2,1)S(1)} collective-permute-done((bf16[256,4224]{1,0:T(8,128)(2,1)S(1)}, bf16[256,4224]{1,0:T(8,128)(2,1)S(1)}, u32[]{:S(2)}, u32[]{:S(2)}) %collective-permute-start.12) | collective-permute-done | bytes 2162720 | tf_op jit(solution)/shard_map/ppermute | solution.py:93
  129.8 0.2 select_reduce_fusion.1
  129.9 1.2 copy-done.13
  131.3 0.1 copy.35.sb_ref
  131.5 0.1 copy.33.sb_ref
  131.6 26.8 %shard_map.75 = (bf16[256,4096]{1,0:T(8,128)(2,1)S(1)}, bf16[256,4096]{1,0:T(8,128)(2,1)}) custom-call(bf16[256,4224]{1,0:T(8,128)(2,1)} %copy-done.10, bf16[256,4224]{1,0:T(8,128)(2,1)} %copy-done.14, f32[256,1]{1,0:T(8,128)S(1)} %copy.32.sa_ref, f32[256,1]{1,0:T(8,128)S(1)} %copy.33.sb_ref, bf16[4096,768]{1,0:T(8,128)(2,1)} %get-tuple-element.70.gate_ref, ...), custom_call_target="tpu_custom_call" | custom-call | flops 9663676416 | bytes 27262976 | tf_op jit(solution)/shard_map/pallas_call | solution.py:47
  158.4 1.3 copy-done
  159.9 1.1 slice.79
  161.0 1.1 slice.80
  162.1 0.3 collective-permute-start.15
  162.4 1.8 collective-permute-start.14
  164.1 26.9 %shard_map.76 = (bf16[256,4096]{1,0:T(8,128)(2,1)S(1)}, bf16[256,4096]{1,0:T(8,128)(2,1)}) custom-call(bf16[256,4224]{1,0:T(8,128)(2,1)} %copy-done.11, bf16[256,4224]{1,0:T(8,128)(2,1)} %copy-done.13, f32[256,1]{1,0:T(8,128)S(1)} %copy.34.sa_ref, f32[256,1]{1,0:T(8,128)S(1)} %copy.35.sb_ref, bf16[4096,768]{1,0:T(8,128)(2,1)} %get-tuple-element.70.gate_ref, ...), custom_call_target="tpu_custom_call" | custom-call | flops 9663676416 | bytes 27262976 | tf_op jit(solution)/shard_map/pallas_call | solution.py:47
  191.1 0.6 collective-permute-start.16
  191.8 0.4 collective-permute-start.7
  192.3 5.6 %collective-permute-done.16.b_ref = bf16[128,4224]{1,0:T(8,128)(2,1)S(1)} collective-permute-done((bf16[128,4224]{1,0:T(8,128)(2,1)S(1)}, bf16[128,4224]{1,0:T(8,128)(2,1)S(1)}, u32[]{:S(2)}, u32[]{:S(2)}) %collective-permute-start.16) | collective-permute-done | bytes 1081376 | tf_op jit(solution)/shard_map/ppermute | solution.py:93
  198.0 1.0 copy-done.4
  199.2 1.2 copy-done.5
  200.5 18.1 %shard_map.77 = (bf16[128,4096]{1,0:T(8,128)(2,1)S(1)}, bf16[128,4096]{1,0:T(8,128)(2,1)S(1)}) custom-call(bf16[128,4224]{1,0:T(8,128)(2,1)S(1)} %constant_dynamic-update-slice_fusion.6.a_ref, bf16[128,4224]{1,0:T(8,128)(2,1)S(1)} %copy-done.5, f32[128,1]{1,0:T(8,128)S(1)} %copy.36.sa_ref, f32[128,1]{1,0:T(8,128)S(1)} %copy.37.sb_ref, ...), custom_call_target="tpu_custom_call" | custom-call | flops 4831838208 | bytes 23068672 | tf_op jit(solution)/shard_map/pallas_call | solution.py:47
  218.6 0.4 collective-permute-start.17
  219.0 2.4 add_convert_fusion
  221.4 0.2 add_convert_fusion.8
  221.8 1.6 collective-permute-start.18
  223.4 0.4 collective-permute-start.22
  223.9 12.0 %collective-permute-done.18 = bf16[64,4096]{1,0:T(8,128)(2,1)S(1)} collective-permute-done((bf16[64,4096]{1,0:T(8,128)(2,1)S(1)}, bf16[64,4096]{1,0:T(8,128)(2,1)S(1)}, u32[]{:S(2)}, u32[]{:S(2)}) %collective-permute-start.18) | collective-permute-done | bytes 524320 | tf_op jit(solution)/shard_map/ppermute | solution.py:87
  235.9 1.3 collective-permute-done.22
  237.2 0.3 add_convert_fusion.11
  237.6 0.5 collective-permute-start.23
  238.1 1.9 collective-permute-start.19
  240.0 2.4 add_convert_fusion.1
  242.4 19.4 %collective-permute-done.23 = bf16[128,4096]{1,0:T(8,128)(2,1)S(1)} collective-permute-done((bf16[128,4096]{1,0:T(8,128)(2,1)S(1)}, bf16[128,4096]{1,0:T(8,128)(2,1)S(1)}, u32[]{:S(2)}, u32[]{:S(2)}) %collective-permute-start.23) | collective-permute-done | bytes 1048608 | tf_op jit(solution)/shard_map/ppermute | solution.py:90
  261.8 0.5 collective-permute-done.19
  262.3 0.8 add_convert_fusion.7
  263.1 1.6 collective-permute-start.20
  264.7 0.4 collective-permute-start.24
  265.2 2.4 add_convert_fusion.2
  267.6 18.6 %collective-permute-done.20 = bf16[128,4096]{1,0:T(8,128)(2,1)S(1)} collective-permute-done((bf16[128,4096]{1,0:T(8,128)(2,1)S(1)}, bf16[128,4096]{1,0:T(8,128)(2,1)S(1)}, u32[]{:S(2)}, u32[]{:S(2)}) %collective-permute-start.20) | collective-permute-done | bytes 1048608 | tf_op jit(solution)/shard_map/ppermute | solution.py:87
  286.2 1.3 collective-permute-done.24
  287.5 0.7 add_convert_fusion.6
  288.2 1.6 collective-permute-start.21
  289.8 0.5 collective-permute-start.25
  290.3 19.8 %collective-permute-done.21 = bf16[128,4096]{1,0:T(8,128)(2,1)S(1)} collective-permute-done((bf16[128,4096]{1,0:T(8,128)(2,1)S(1)}, bf16[128,4096]{1,0:T(8,128)(2,1)S(1)}, u32[]{:S(2)}, u32[]{:S(2)}) %collective-permute-start.21) | collective-permute-done | bytes 1048608 | tf_op jit(solution)/shard_map/ppermute | solution.py:87
  310.0 1.3 collective-permute-done.25
  311.3 2.9 add_convert_fusion.3
  (65 shorter events, 2.2 us)
Async XLA Ops:
  3.2 27.0 %collective-permute-start = (bf16[128,4224]{1,0:T(8,128)(2,1)S(1)}, bf16[128,4224]{1,0:T(8,128)(2,1)}, u32[]{:S(2)}, u32[]{:S(2)}) collective-permute-start(bf16[128,4224]{1,0:T(8,128)(2,1)S(1)} %pad_maximum_fusion.a_ref), channel_id=1, source_target_pairs={{0,4},{1,5},{4,8},{5,9},{8,12},{9,13},{12,14},{13,15},{14,10},{15,... | collective-permute-start | bytes 3244040 | tf_op jit(solution)/shard_map/ppermute | solution.py:87
  6.3 26.2 %collective-permute-start.1 = (bf16[128,4224]{1,0:T(8,128)(2,1)S(1)}, bf16[128,4224]{1,0:T(8,128)(2,1)}, u32[]{:S(2)}, u32[]{:S(2)}) collective-permute-start(bf16[128,4224]{1,0:T(8,128)(2,1)S(1)} %pad_maximum_fusion.a_ref), channel_id=1, source_target_pairs={{4,0},{5,1},{8,4},{9,5},{12,8},{13,9},{14,12},{15,13},{10,14},{11,... | collective-permute-start | bytes 3244040 | tf_op jit(solution)/shard_map/ppermute | solution.py:90
  6.3 39.7 %collective-permute-start.2 = (bf16[128,4224]{1,0:T(8,128)(2,1)S(1)}, bf16[128,4224]{1,0:T(8,128)(2,1)S(1)}, u32[]{:S(2)}, u32[]{:S(2)}) collective-permute-start(bf16[128,4224]{1,0:T(8,128)(2,1)S(1)} %pad_maximum_fusion.a_ref), channel_id=1, source_target_pairs={{0,1},{1,0},{2,3},{3,2},{4,5},{5,4},{6,7},{7,6},{8,9},{9,8},{10,11... | collective-permute-start | bytes 3244040 | tf_op jit(solution)/shard_map/ppermute | solution.py:93
  6.3 28.5 %copy-start.12 = (f32[4096]{0:T(1024)S(1)}, f32[4096]{0:T(1024)}, u32[]{:S(2)}) copy-start(f32[4096]{0:T(1024)} %param.10) | copy-start | bytes 49156
  34.8 33.5 %collective-permute-start.6 = (bf16[256,4224]{1,0:T(8,128)(2,1)}, bf16[256,4224]{1,0:T(8,128)(2,1)}, u32[]{:S(2)}, u32[]{:S(2)}) collective-permute-start(bf16[256,4224]{1,0:T(8,128)(2,1)} %constant_dynamic-update-slice_fusion.a_ref), channel_id=1, source_target_pairs={{0,1},{1,0},{2,3},{3,2},{4,5},{5,4},{6,7},{7,6},{8,9},{9,8},{10,11... | collective-permute-start | bytes 6488072 | tf_op jit(solution)/shard_map/ppermute | solution.py:93
  65.3 1.0 copy-start.6
  66.3 30.1 %collective-permute-start.4 = (bf16[128,4224]{1,0:T(8,128)(2,1)}, bf16[128,4224]{1,0:T(8,128)(2,1)}, u32[]{:S(2)}, u32[]{:S(2)}) collective-permute-start(bf16[128,4224]{1,0:T(8,128)(2,1)} %collective-permute-done), channel_id=1, source_target_pairs={{0,4},{1,5},{4,8},{5,9},{8,12},{9,13},{12,14},{13,15},{14,10},{15,... | collective-permute-start | bytes 3244040 | tf_op jit(solution)/shard_map/ppermute | solution.py:87
  68.1 28.3 %collective-permute-start.5 = (bf16[128,4224]{1,0:T(8,128)(2,1)}, bf16[128,4224]{1,0:T(8,128)(2,1)S(1)}, u32[]{:S(2)}, u32[]{:S(2)}) collective-permute-start(bf16[128,4224]{1,0:T(8,128)(2,1)} %collective-permute-done.1), channel_id=1, source_target_pairs={{4,0},{5,1},{8,4},{9,5},{12,8},{13,9},{14,12},{15,13},{10,14},{11,... | collective-permute-start | bytes 3244040 | tf_op jit(solution)/shard_map/ppermute | solution.py:90
  96.4 26.0 %collective-permute-start.8 = (bf16[128,4224]{1,0:T(8,128)(2,1)}, bf16[128,4224]{1,0:T(8,128)(2,1)S(1)}, u32[]{:S(2)}, u32[]{:S(2)}) collective-permute-start(bf16[128,4224]{1,0:T(8,128)(2,1)} %collective-permute-done.4), channel_id=1, source_target_pairs={{0,4},{1,5},{4,8},{5,9},{8,12},{9,13},{12,14},{13,15},{14,10},{15,... | collective-permute-start | bytes 3244040 | tf_op jit(solution)/shard_map/ppermute | solution.py:87
  99.6 25.7 %collective-permute-start.9 = (bf16[128,4224]{1,0:T(8,128)(2,1)S(1)}, bf16[128,4224]{1,0:T(8,128)(2,1)S(1)}, u32[]{:S(2)}, u32[]{:S(2)}) collective-permute-start(bf16[128,4224]{1,0:T(8,128)(2,1)S(1)} %collective-permute-done.5), channel_id=1, source_target_pairs={{4,0},{5,1},{8,4},{9,5},{12,8},{13,9},{14,12},{15,13},{10,14},{11,... | collective-permute-start | bytes 3244040 | tf_op jit(solution)/shard_map/ppermute | solution.py:90
  100.2 29.6 %copy-start.10 = (bf16[256,4224]{1,0:T(8,128)(2,1)}, bf16[256,4224]{1,0:T(8,128)(2,1)S(1)}, u32[]{:S(2)}) copy-start(bf16[256,4224]{1,0:T(8,128)(2,1)S(1)} %constant_dynamic-update-slice_fusion.2.a_ref) | copy-start | bytes 6488068
  100.2 25.3 %collective-permute-start.10 = (bf16[256,4224]{1,0:T(8,128)(2,1)S(1)}, bf16[256,4224]{1,0:T(8,128)(2,1)S(1)}, u32[]{:S(2)}, u32[]{:S(2)}) collective-permute-start(bf16[256,4224]{1,0:T(8,128)(2,1)S(1)} %constant_dynamic-update-slice_fusion.2.a_ref), channel_id=1, source_target_pairs={{0,1},{1,0},{2,3},{3,2},{4,5},{5,4},{6,7},{7,6},{8,9},{9,8},{10,11... | collective-permute-start | bytes 6488072 | tf_op jit(solution)/shard_map/ppermute | solution.py:93
  122.4 3.0 copy-start.8
  125.3 4.6 %copy-start.9 = (bf16[128,4224]{1,0:T(8,128)(2,1)}, bf16[128,4224]{1,0:T(8,128)(2,1)S(1)}, u32[]{:S(2)}) copy-start(bf16[128,4224]{1,0:T(8,128)(2,1)S(1)} %collective-permute-done.9) | copy-start | bytes 3244036
  125.4 4.5 %copy-start.11 = (bf16[256,4224]{1,0:T(8,128)(2,1)}, bf16[256,4224]{1,0:T(8,128)(2,1)S(1)}, u32[]{:S(2)}) copy-start(bf16[256,4224]{1,0:T(8,128)(2,1)S(1)} %constant_dynamic-update-slice_fusion.4.a_ref) | copy-start | bytes 6488068
  125.4 4.3 %collective-permute-start.12 = (bf16[256,4224]{1,0:T(8,128)(2,1)S(1)}, bf16[256,4224]{1,0:T(8,128)(2,1)S(1)}, u32[]{:S(2)}, u32[]{:S(2)}) collective-permute-start(bf16[256,4224]{1,0:T(8,128)(2,1)S(1)} %constant_dynamic-update-slice_fusion.4.a_ref), channel_id=1, source_target_pairs={{0,1},{1,0},{2,3},{3,2},{4,5},{5,4},{6,7},{7,6},{8,9},{9,8},{10,11... | collective-permute-start | bytes 6488072 | tf_op jit(solution)/shard_map/ppermute | solution.py:93
  125.5 4.4 %copy-start.14 = (bf16[256,4224]{1,0:T(8,128)(2,1)}, bf16[256,4224]{1,0:T(8,128)(2,1)S(1)}, u32[]{:S(2)}) copy-start(bf16[256,4224]{1,0:T(8,128)(2,1)S(1)} %collective-permute-done.10.b_ref) | copy-start | bytes 6488068
  129.8 1.4 copy-start.13
  158.4 1.3 copy-start
  162.1 29.0 %collective-permute-start.15 = (bf16[64,4224]{1,0:T(8,128)(2,1)S(1)}, bf16[64,4224]{1,0:T(8,128)(2,1)S(1)}, u32[]{:S(2)}, u32[]{:S(2)}) collective-permute-start(bf16[64,4224]{1,0:T(8,128)(2,1)S(1)} %slice.80), channel_id=1, source_target_pairs={{4,0},{5,1},{8,4},{9,5},{12,8},{13,9},{14,12},{15,13},{10,14},{11,... | collective-permute-start | bytes 1622024 | tf_op jit(solution)/shard_map/ppermute | solution.py:90
  162.4 28.6 %collective-permute-start.14 = (bf16[64,4224]{1,0:T(8,128)(2,1)S(1)}, bf16[64,4224]{1,0:T(8,128)(2,1)S(1)}, u32[]{:S(2)}, u32[]{:S(2)}) collective-permute-start(bf16[64,4224]{1,0:T(8,128)(2,1)S(1)} %slice.79), channel_id=1, source_target_pairs={{0,4},{1,5},{4,8},{5,9},{8,12},{9,13},{12,14},{13,15},{14,10},{15,... | collective-permute-start | bytes 1622024 | tf_op jit(solution)/shard_map/ppermute | solution.py:87
  191.0 6.9 %copy-start.2 = (bf16[256,4096]{1,0:T(8,128)(2,1)}, bf16[256,4096]{1,0:T(8,128)(2,1)S(1)}, u32[]{:S(2)}) copy-start(bf16[256,4096]{1,0:T(8,128)(2,1)S(1)} %get-tuple-element.43) | copy-start | bytes 6291460
  191.0 28.0 %collective-permute-start.13 = (bf16[256,4096]{1,0:T(8,128)(2,1)}, bf16[256,4096]{1,0:T(8,128)(2,1)}, u32[]{:S(2)}, u32[]{:S(2)}) collective-permute-start(bf16[256,4096]{1,0:T(8,128)(2,1)} %get-tuple-element.44), channel_id=1, source_target_pairs={{0,1},{1,0},{2,3},{3,2},{4,5},{5,4},{6,7},{7,6},{8,9},{9,8},{10,11... | collective-permute-start | bytes 6291464 | tf_op jit(solution)/shard_map/ppermute | solution.py:93
  191.1 6.8 %collective-permute-start.16 = (bf16[128,4224]{1,0:T(8,128)(2,1)S(1)}, bf16[128,4224]{1,0:T(8,128)(2,1)S(1)}, u32[]{:S(2)}, u32[]{:S(2)}) collective-permute-start(bf16[128,4224]{1,0:T(8,128)(2,1)S(1)} %constant_dynamic-update-slice_fusion.6.a_ref), channel_id=1, source_target_pairs={{0,1},{1,0},{2,3},{3,2},{4,5},{5,4},{6,7},{7,6},{8,9},{9,8},{10,11... | collective-permute-start | bytes 3244040 | tf_op jit(solution)/shard_map/ppermute | solution.py:93
  191.7 98.6 %collective-permute-start.3 = (bf16[128,4096]{1,0:T(8,128)(2,1)}, bf16[128,4096]{1,0:T(8,128)(2,1)}, u32[]{:S(2)}, u32[]{:S(2)}) collective-permute-start(bf16[128,4096]{1,0:T(8,128)(2,1)} %get-tuple-element.30), channel_id=1, source_target_pairs={{0,1},{1,0},{2,3},{3,2},{4,5},{5,4},{6,7},{7,6},{8,9},{9,8},{10,11... | collective-permute-start | bytes 3145736 | tf_op jit(solution)/shard_map/ppermute | solution.py:93
  191.8 73.4 %collective-permute-start.7 = (bf16[256,4096]{1,0:T(8,128)(2,1)}, bf16[256,4096]{1,0:T(8,128)(2,1)}, u32[]{:S(2)}, u32[]{:S(2)}) collective-permute-start(bf16[256,4096]{1,0:T(8,128)(2,1)} %get-tuple-element.36), channel_id=1, source_target_pairs={{0,1},{1,0},{2,3},{3,2},{4,5},{5,4},{6,7},{7,6},{8,9},{9,8},{10,11... | collective-permute-start | bytes 6291464 | tf_op jit(solution)/shard_map/ppermute | solution.py:93
  192.2 47.8 %collective-permute-start.11 = (bf16[256,4096]{1,0:T(8,128)(2,1)}, bf16[256,4096]{1,0:T(8,128)(2,1)}, u32[]{:S(2)}, u32[]{:S(2)}) collective-permute-start(bf16[256,4096]{1,0:T(8,128)(2,1)} %get-tuple-element.42), channel_id=1, source_target_pairs={{0,1},{1,0},{2,3},{3,2},{4,5},{5,4},{6,7},{7,6},{8,9},{9,8},{10,11... | collective-permute-start | bytes 6291464 | tf_op jit(solution)/shard_map/ppermute | solution.py:93
  198.0 1.0 copy-start.4
  199.2 1.2 copy-start.5
  200.5 18.6 %copy-start.3 = (bf16[256,4096]{1,0:T(8,128)(2,1)S(1)}, bf16[256,4096]{1,0:T(8,128)(2,1)}, u32[]{:S(2)}) copy-start(bf16[256,4096]{1,0:T(8,128)(2,1)} %copy-done.2) | copy-start | bytes 6291460
  218.6 2.8 collective-permute-start.17
  221.8 14.1 %collective-permute-start.18 = (bf16[64,4096]{1,0:T(8,128)(2,1)S(1)}, bf16[64,4096]{1,0:T(8,128)(2,1)S(1)}, u32[]{:S(2)}, u32[]{:S(2)}) collective-permute-start(bf16[64,4096]{1,0:T(8,128)(2,1)S(1)} %get-tuple-element.67), channel_id=1, source_target_pairs={{0,4},{1,5},{4,8},{5,9},{8,12},{9,13},{12,14},{13,15},{14,10},{15,... | collective-permute-start | bytes 1572872 | tf_op jit(solution)/shard_map/ppermute | solution.py:87
  223.4 13.8 %collective-permute-start.22 = (bf16[64,4096]{1,0:T(8,128)(2,1)S(1)}, bf16[64,4096]{1,0:T(8,128)(2,1)S(1)}, u32[]{:S(2)}, u32[]{:S(2)}) collective-permute-start(bf16[64,4096]{1,0:T(8,128)(2,1)S(1)} %get-tuple-element.68), channel_id=1, source_target_pairs={{4,0},{5,1},{8,4},{9,5},{12,8},{13,9},{14,12},{15,13},{10,14},{11,... | collective-permute-start | bytes 1572872 | tf_op jit(solution)/shard_map/ppermute | solution.py:90
  237.5 2.5 copy-start.1
  237.6 24.2 %collective-permute-start.23 = (bf16[128,4096]{1,0:T(8,128)(2,1)S(1)}, bf16[128,4096]{1,0:T(8,128)(2,1)S(1)}, u32[]{:S(2)}, u32[]{:S(2)}) collective-permute-start(bf16[128,4096]{1,0:T(8,128)(2,1)S(1)} %pad_maximum_fusion.2), channel_id=1, source_target_pairs={{4,0},{5,1},{8,4},{9,5},{12,8},{13,9},{14,12},{15,13},{10,14},{11,... | collective-permute-start | bytes 3145736 | tf_op jit(solution)/shard_map/ppermute | solution.py:90
  238.1 24.2 %collective-permute-start.19 = (bf16[128,4096]{1,0:T(8,128)(2,1)S(1)}, bf16[128,4096]{1,0:T(8,128)(2,1)S(1)}, u32[]{:S(2)}, u32[]{:S(2)}) collective-permute-start(bf16[128,4096]{1,0:T(8,128)(2,1)S(1)} %pad_maximum_fusion.1), channel_id=1, source_target_pairs={{0,4},{1,5},{4,8},{5,9},{8,12},{9,13},{12,14},{13,15},{14,10},{15,... | collective-permute-start | bytes 3145736 | tf_op jit(solution)/shard_map/ppermute | solution.py:87
  263.1 23.0 %collective-permute-start.20 = (bf16[128,4096]{1,0:T(8,128)(2,1)S(1)}, bf16[128,4096]{1,0:T(8,128)(2,1)S(1)}, u32[]{:S(2)}, u32[]{:S(2)}) collective-permute-start(bf16[128,4096]{1,0:T(8,128)(2,1)S(1)} %get-tuple-element.61), channel_id=1, source_target_pairs={{0,4},{1,5},{4,8},{5,9},{8,12},{9,13},{12,14},{13,15},{14,10},{15,... | collective-permute-start | bytes 3145736 | tf_op jit(solution)/shard_map/ppermute | solution.py:87
  264.7 22.7 %collective-permute-start.24 = (bf16[128,4096]{1,0:T(8,128)(2,1)S(1)}, bf16[128,4096]{1,0:T(8,128)(2,1)S(1)}, u32[]{:S(2)}, u32[]{:S(2)}) collective-permute-start(bf16[128,4096]{1,0:T(8,128)(2,1)S(1)} %get-tuple-element.62), channel_id=1, source_target_pairs={{4,0},{5,1},{8,4},{9,5},{12,8},{13,9},{14,12},{15,13},{10,14},{11,... | collective-permute-start | bytes 3145736 | tf_op jit(solution)/shard_map/ppermute | solution.py:90
  267.6 43.7 %copy-start.7 = (bf16[128,4096]{1,0:T(8,128)(2,1)S(1)}, bf16[128,4096]{1,0:T(8,128)(2,1)}, u32[]{:S(2)}) copy-start(bf16[128,4096]{1,0:T(8,128)(2,1)} %copy-done.6) | copy-start | bytes 3145732
  288.2 21.8 %collective-permute-start.21 = (bf16[128,4096]{1,0:T(8,128)(2,1)S(1)}, bf16[128,4096]{1,0:T(8,128)(2,1)S(1)}, u32[]{:S(2)}, u32[]{:S(2)}) collective-permute-start(bf16[128,4096]{1,0:T(8,128)(2,1)S(1)} %get-tuple-element.59), channel_id=1, source_target_pairs={{0,4},{1,5},{4,8},{5,9},{8,12},{9,13},{12,14},{13,15},{14,10},{15,... | collective-permute-start | bytes 3145736 | tf_op jit(solution)/shard_map/ppermute | solution.py:87
  289.8 21.5 %collective-permute-start.25 = (bf16[128,4096]{1,0:T(8,128)(2,1)S(1)}, bf16[128,4096]{1,0:T(8,128)(2,1)S(1)}, u32[]{:S(2)}, u32[]{:S(2)}) collective-permute-start(bf16[128,4096]{1,0:T(8,128)(2,1)S(1)} %get-tuple-element.60), channel_id=1, source_target_pairs={{4,0},{5,1},{8,4},{9,5},{12,8},{13,9},{14,12},{15,13},{10,14},{11,... | collective-permute-start | bytes 3145736 | tf_op jit(solution)/shard_map/ppermute | solution.py:90
where the time goes:
time: 315 us; the launch traced here: 314 us
  waiting for transfers between devices  133 us (42%)
  Pallas kernels  118 us (37%)
  other arithmetic  26.3 us (8%)
  starting transfers between devices  19.8 us (6%)
  local copies, waits for them, and re-layouts  17.3 us (5%)
    pallas_call x5, Pallas kernels, ffn(): pl.pallas_call(ffn_body, grid=(steps,), in_specs=[pl.BlockSpec((rows, wid...  118 us
    ppermute x8, waiting for transfers between devices, fwd(): return lax.ppermute(x, 'ep', forward)  96.9 us
    ppermute x8, waiting for transfers between devices, bwd(): return lax.ppermute(x, 'ep', backward)  26.1 us
    ppermute x8, starting transfers between devices, fwd(): return lax.ppermute(x, 'ep', forward)  15.2 us
    convert_element_type x8, other arithmetic, add(): return total.astype(jnp.bfloat16)  11.9 us
    convert_element_type x1, other arithmetic, shards(): (smooth[:, None] * up_weight[0].astype(jnp.float32)).astype(jnp.bfloat16)  11.2 us
    unnamed x35, local copies, waits for them, and re-layouts  10.3 us
    ppermute x10, waiting for transfers between devices, other(): return lax.ppermute(x, 'ep', swap)  9.84 us
  transfers between devices with their start and end apart: 26, of which 13 were waited for; matrix products, arithmetic and copies ran while one was open for 9% of the time, Pallas kernels for 29%

commit v1 on v0

--- a/solution.py
+++ b/solution.py
@@ -113,42 +113,46 @@
             total = total + x.astype(jnp.float32)
         return total.astype(jnp.bfloat16)
 
-    def compute(*blocks):
+    def pair(*blocks):
         mine = jnp.concatenate(blocks, axis=0) if len(blocks) > 1 else blocks[0]
-        theirs = other(mine)
-        return ffn(
+        return mine, other(mine)
+
+    def compute(mine, theirs):
+        kept, sent = ffn(
             mine, theirs, scale_of(mine), scale_of(theirs), folded_gate, folded_up, down_one
         )
+        return add(kept, other(sent))
 
-    behind, ahead = [own], [own]
-    parts = [compute(own)]
+    x, y = own, own
+    pairs = [pair(own)]
+    near = None
     for d in range(1, far + 1):
-        x, y = behind[-1], ahead[-1]
-        if d >= 2:
-            x, y, parts[d - 2] = lax.optimization_barrier((x, y, parts[d - 2]))
         if d == far:
             x, y = x[:half], y[half:]
-        behind.append(fwd(x))
-        ahead.append(bwd(y))
-        parts.append(compute(behind[d], ahead[d]))
+        x, y = fwd(x), bwd(y)
+        pairs.append(pair(x, y))
+        if d == 1:
+            near = compute(*pairs[1])
+    last = compute(*pairs[far])
 
-    sums = [add(p[0], other(p[1])) for p in parts]
-    here, last = sums[0], sums[far]
-    to_behind = {d: sums[d][:tok_dev] for d in range(1, far)}
-    to_ahead = {d: sums[d][tok_dev:] for d in range(1, far)}
-
-    up_sum = fwd(last[:half])
-    down_sum = bwd(last[half:])
+    up_sum, down_sum = last[:half], last[half:]
+    here = None
     for d in range(far - 1, 0, -1):
+        mine, theirs = pairs[d] if d > 1 else pairs[0]
+        mine, theirs, up_sum, down_sum = lax.optimization_barrier(
+            (mine, theirs, up_sum, down_sum)
+        )
+        both = compute(mine, theirs)
+        if d == 1:
+            here, both = both, near
+        b, a = both[:tok_dev], both[tok_dev:]
+        up_sum, down_sum = fwd(up_sum), bwd(down_sum)
         if d == far - 1:
-            a, b = to_ahead[d], to_behind[d]
             up_sum = jnp.concatenate([add(a[:half], up_sum), a[half:]], axis=0)
             down_sum = jnp.concatenate([b[:half], add(b[half:], down_sum)], axis=0)
         else:
-            up_sum = add(to_ahead[d], up_sum)
-            down_sum = add(to_behind[d], down_sum)
-        up_sum, down_sum = fwd(up_sum), bwd(down_sum)
-    return add(here, up_sum, down_sum)
+            up_sum, down_sum = add(a, up_sum), add(b, down_sum)
+    return add(here, fwd(up_sum), bwd(down_sum))
 
 
 def solution(mesh):

time: 315 us -> 320 us (1.016)
  waiting for transfers between devices: 133 us -> 145 us
  local copies, waits for them, and re-layouts: 17.3 us -> 13.7 us
    ppermute x8, waiting for transfers between devices: 96.9 us -> 124 us  [fwd(): return lax.ppermute(x, 'ep', forward)]
    ppermute x8, waiting for transfers between devices: 26.1 us -> 13.5 us  [bwd(): return lax.ppermute(x, 'ep', backward)]
    unnamed x35 -> x55, local copies, waits for them, and re-layouts: 10.3 us -> 10.2 us
  transfers between devices with their start and end apart: 26 -> 26, of which waited for: 13 -> 17; matrix products, arithmetic and copies ran while one was open for 9% -> 8% of each run, Pallas kernels for 29% -> 14%
where the time goes in v1:
time: 320 us; the launch traced here: 319 us
  waiting for transfers between devices  145 us (45%)
  Pallas kernels  115 us (36%)
  other arithmetic  25.3 us (8%)
  starting transfers between devices  20 us (6%)
  local copies, waits for them, and re-layouts  13.7 us (4%)
    ppermute x8, waiting for transfers between devices, fwd(): return lax.ppermute(x, 'ep', forward)  124 us
    pallas_call x5, Pallas kernels, ffn(): pl.pallas_call(ffn_body, grid=(steps,), in_specs=[pl.BlockSpec((rows, wid...  115 us
    ppermute x8, waiting for transfers between devices, bwd(): return lax.ppermute(x, 'ep', backward)  13.5 us
    ppermute x8, starting transfers between devices, fwd(): return lax.ppermute(x, 'ep', forward)  13 us
    convert_element_type x1, other arithmetic, shards(): (smooth[:, None] * up_weight[0].astype(jnp.float32)).astype(jnp.bfloat16)  11.1 us
    convert_element_type x8, other arithmetic, add(): return total.astype(jnp.bfloat16)  10.4 us
    unnamed x55, local copies, waits for them, and re-layouts  10.2 us
    ppermute x10, waiting for transfers between devices, other(): return lax.ppermute(x, 'ep', swap)  8.15 us
  transfers between devices with their start and end apart: 26, of which 17 were waited for; matrix products, arithmetic and copies ran while one was open for 8% of the time, Pallas kernels for 14%

profile of v1, /device:TPU:0, one launch (start us, length us, event | category | flops | bytes accessed | tf_op | source)
XLA Modules:
  0.0 319.3 jit_solution(9534120749752851259)
XLA Ops:
  0.0 0.8 copy.26
  0.8 0.8 copy.27
  1.6 0.4 select_reduce_fusion
  1.9 1.3 pad_maximum_fusion.a_ref
  3.3 3.1 collective-permute-start.1
  6.4 23.8 %collective-permute-done.1 = bf16[128,4224]{1,0:T(8,128)(2,1)S(1)} collective-permute-done((bf16[128,4224]{1,0:T(8,128)(2,1)S(1)}, bf16[128,4224]{1,0:T(8,128)(2,1)S(1)}, u32[]{:S(2)}, u32[]{:S(2)}) %collective-permute-start.1) | collective-permute-done | bytes 1081376 | tf_op jit(solution)/shard_map/ppermute | solution.py:87
  30.2 1.8 collective-permute-start.2
  32.0 0.2 collective-permute-start.4
  32.2 23.0 %collective-permute-done.2 = bf16[128,4224]{1,0:T(8,128)(2,1)S(1)} collective-permute-done((bf16[128,4224]{1,0:T(8,128)(2,1)S(1)}, bf16[128,4224]{1,0:T(8,128)(2,1)S(1)}, u32[]{:S(2)}, u32[]{:S(2)}) %collective-permute-start.2) | collective-permute-done | bytes 1081376 | tf_op jit(solution)/shard_map/ppermute | solution.py:87
  55.2 1.5 collective-permute-start.6
  56.7 0.9 collective-permute-start.7
  57.6 21.7 %collective-permute-done.6 = bf16[128,4224]{1,0:T(8,128)(2,1)S(1)} collective-permute-done((bf16[128,4224]{1,0:T(8,128)(2,1)S(1)}, bf16[128,4224]{1,0:T(8,128)(2,1)S(1)}, u32[]{:S(2)}, u32[]{:S(2)}) %collective-permute-start.6) | collective-permute-done | bytes 1081376 | tf_op jit(solution)/shard_map/ppermute | solution.py:87
  79.3 1.0 copy-done.4
  80.3 0.8 slice.94
  81.2 1.2 collective-permute-start.9
  82.3 11.1 %fusion = (bf16[4096,768]{1,0:T(8,128)(2,1)}, bf16[4096,768]{1,0:T(8,128)(2,1)}) fusion(bf16[1,4096,768]{2,1,0:T(8,128)(2,1)} %param.12, f32[4096]{0:T(1024)S(1)} %copy-done.21, bf16[1,4096,768]{2,1,0:T(8,128)(2,1)} %param.11), kind=kLoop, calls=%fused_computation.1 | loop fusion | flops 18874368 | bytes 25182208 | tf_op jit(solution)/shard_map/convert_element_type | solution.py:102
  93.6 1.1 collective-permute-start.10
  94.7 1.1 constant_dynamic-update-slice_fusion.5
  95.8 9.1 %collective-permute-done.10 = bf16[64,4224]{1,0:T(8,128)(2,1)S(1)} collective-permute-done((bf16[64,4224]{1,0:T(8,128)(2,1)S(1)}, bf16[64,4224]{1,0:T(8,128)(2,1)S(1)}, u32[]{:S(2)}, u32[]{:S(2)}) %collective-permute-start.10) | collective-permute-done | bytes 540704 | tf_op jit(solution)/shard_map/ppermute | solution.py:90
  105.0 1.1 constant_dynamic-update-slice_fusion.7
  106.0 1.1 constant_dynamic-update-slice_fusion.3
  107.1 0.5 collective-permute-done.11.b_ref
  108.0 18.1 %shard_map.73 = (bf16[128,4096]{1,0:T(8,128)(2,1)S(1)}, bf16[128,4096]{1,0:T(8,128)(2,1)S(1)}) custom-call(bf16[128,4224]{1,0:T(8,128)(2,1)S(1)} %constant_dynamic-update-slice_fusion.4.a_ref, bf16[128,4224]{1,0:T(8,128)(2,1)S(1)} %collective-permute-done.11.b_ref, f32[128,1]{1,0:T(8,128)S(1)} %copy.28.sa_ref, f32[128,1]{1,0:T(8,128)S(1)} %copy.29.sb_ref, ...), custom_call_target="tpu_custom_call" | custom-call | flops 4831838208 | bytes 23068672 | tf_op jit(solution)/shard_map/pallas_call | solution.py:47
  126.5 0.4 collective-permute-start.8
  127.0 0.4 copy-done.11
  127.5 0.2 collective-permute-start.20
  127.7 1.1 collective-permute-done.12
  128.9 0.2 add_convert_fusion.9
  129.2 2.8 collective-permute-done.8.b_ref
  132.0 3.1 collective-permute-done.20.b_ref
  135.3 1.2 copy-done.23
  136.7 25.6 %shard_map.74 = (bf16[256,4096]{1,0:T(8,128)(2,1)S(1)}, bf16[256,4096]{1,0:T(8,128)(2,1)S(1)}) custom-call(bf16[256,4224]{1,0:T(8,128)(2,1)} %copy-done.19, bf16[256,4224]{1,0:T(8,128)(2,1)} %copy-done.24, f32[256,1]{1,0:T(8,128)S(1)} %copy.30.sa_ref, f32[256,1]{1,0:T(8,128)S(1)} %copy.31.sb_ref, bf16[4096,768]{1,0:T(8,128)(2,1)} %get-tuple-element.70.gate_ref, ...), custom_call_target="tpu_custom_call" | custom-call | flops 9663676416 | bytes 27262976 | tf_op jit(solution)/shard_map/pallas_call | solution.py:47
  162.6 0.9 copy-done.9
  163.9 1.6 collective-permute-start.14
  165.5 0.4 collective-permute-start.15
  166.0 0.6 collective-permute-done.13
  166.6 0.8 add_convert_fusion.2
  167.5 10.7 %collective-permute-done.14 = bf16[64,4096]{1,0:T(8,128)(2,1)S(1)} collective-permute-done((bf16[64,4096]{1,0:T(8,128)(2,1)S(1)}, bf16[64,4096]{1,0:T(8,128)(2,1)S(1)}, u32[]{:S(2)}, u32[]{:S(2)}) %collective-permute-start.14) | collective-permute-done | bytes 524320 | tf_op jit(solution)/shard_map/ppermute | solution.py:87
  178.1 1.3 collective-permute-done.15
  179.4 0.2 add_convert_fusion.10
  179.7 1.6 pad_maximum_fusion.1
  181.4 1.2 copy-done.22
  182.9 27.2 %shard_map.75 = (bf16[256,4096]{1,0:T(8,128)(2,1)S(1)}, bf16[256,4096]{1,0:T(8,128)(2,1)}) custom-call(bf16[256,4224]{1,0:T(8,128)(2,1)} %copy-done.20, bf16[256,4224]{1,0:T(8,128)(2,1)} %copy-done.22, f32[256,1]{1,0:T(8,128)S(1)} %copy.32.sa_ref, f32[256,1]{1,0:T(8,128)S(1)} %copy.33.sb_ref, bf16[4096,768]{1,0:T(8,128)(2,1)} %get-tuple-element.70.gate_ref, ...), custom_call_target="tpu_custom_call" | custom-call | flops 9663676416 | bytes 27262976 | tf_op jit(solution)/shard_map/pallas_call | solution.py:47
  210.4 25.7 %shard_map.77 = (bf16[256,4096]{1,0:T(8,128)(2,1)S(1)}, bf16[256,4096]{1,0:T(8,128)(2,1)S(1)}) custom-call(bf16[256,4224]{1,0:T(8,128)(2,1)} %copy-done.17, bf16[256,4224]{1,0:T(8,128)(2,1)} %copy-done.23, f32[256,1]{1,0:T(8,128)S(1)} %copy.36.sa_ref, f32[256,1]{1,0:T(8,128)S(1)} %copy.37.sb_ref, bf16[4096,768]{1,0:T(8,128)(2,1)} %get-tuple-element.70.gate_ref, ...), custom_call_target="tpu_custom_call" | custom-call | flops 9663676416 | bytes 27262976 | tf_op jit(solution)/shard_map/pallas_call | solution.py:47
  236.0 0.6 collective-permute-start.21
  236.7 1.6 collective-permute-start.17
  238.2 0.4 collective-permute-start.18
  238.7 2.4 add_convert_fusion.1
  241.1 21.1 %collective-permute-done.17 = bf16[128,4096]{1,0:T(8,128)(2,1)S(1)} collective-permute-done((bf16[128,4096]{1,0:T(8,128)(2,1)S(1)}, bf16[128,4096]{1,0:T(8,128)(2,1)S(1)}, u32[]{:S(2)}, u32[]{:S(2)}) %collective-permute-start.17) | collective-permute-done | bytes 1048608 | tf_op jit(solution)/shard_map/ppermute | solution.py:87
  262.2 1.3 collective-permute-done.18
  263.5 2.1 add_convert_fusion.7
  265.6 1.5 collective-permute-start.22
  267.1 0.5 collective-permute-start.24
  267.6 0.8 add_convert_fusion
  268.8 1.2 copy-done.1
  270.0 18.0 %shard_map.76 = (bf16[128,4096]{1,0:T(8,128)(2,1)S(1)}, bf16[128,4096]{1,0:T(8,128)(2,1)S(1)}) custom-call(bf16[128,4224]{1,0:T(8,128)(2,1)S(1)} %pad_maximum_fusion.a_ref, bf16[128,4224]{1,0:T(8,128)(2,1)S(1)} %copy-done.1, f32[128,1]{1,0:T(8,128)S(1)} %copy.34.sa_ref, f32[128,1]{1,0:T(8,128)S(1)} %copy.35.sb_ref, ...), custom_call_target="tpu_custom_call" | custom-call | flops 4831838208 | bytes 23068672 | tf_op jit(solution)/shard_map/pallas_call | solution.py:47
  288.1 2.2 collective-permute-done.22
  290.3 1.2 collective-permute-done.24
  291.5 2.3 add_convert_fusion.5
  293.9 0.8 collective-permute-start.23
  294.6 1.3 collective-permute-start.25
  295.9 21.2 %collective-permute-done.23 = bf16[128,4096]{1,0:T(8,128)(2,1)S(1)} collective-permute-done((bf16[128,4096]{1,0:T(8,128)(2,1)S(1)}, bf16[128,4096]{1,0:T(8,128)(2,1)S(1)}, u32[]{:S(2)}, u32[]{:S(2)}) %collective-permute-start.23) | collective-permute-done | bytes 1048608 | tf_op jit(solution)/shard_map/ppermute | solution.py:87
  317.1 0.6 collective-permute-done.25
  317.7 1.6 add_convert_fusion.3
  (84 shorter events, 3.4 us)
Async XLA Ops:
  0.0 82.3 %copy-start.21 = (f32[4096]{0:T(1024)S(1)}, f32[4096]{0:T(1024)}, u32[]{:S(2)}) copy-start(f32[4096]{0:T(1024)} %param.10) | copy-start | bytes 49156
  3.3 26.9 %collective-permute-start.1 = (bf16[128,4224]{1,0:T(8,128)(2,1)S(1)}, bf16[128,4224]{1,0:T(8,128)(2,1)S(1)}, u32[]{:S(2)}, u32[]{:S(2)}) collective-permute-start(bf16[128,4224]{1,0:T(8,128)(2,1)S(1)} %pad_maximum_fusion.a_ref), channel_id=1, source_target_pairs={{0,4},{1,5},{4,8},{5,9},{8,12},{9,13},{12,14},{13,15},{14,10},{15,... | collective-permute-start | bytes 3244040 | tf_op jit(solution)/shard_map/ppermute | solution.py:87
  6.3 25.6 %collective-permute-start.3 = (bf16[128,4224]{1,0:T(8,128)(2,1)S(1)}, bf16[128,4224]{1,0:T(8,128)(2,1)S(1)}, u32[]{:S(2)}, u32[]{:S(2)}) collective-permute-start(bf16[128,4224]{1,0:T(8,128)(2,1)S(1)} %pad_maximum_fusion.a_ref), channel_id=1, source_target_pairs={{4,0},{5,1},{8,4},{9,5},{12,8},{13,9},{14,12},{15,13},{10,14},{11,... | collective-permute-start | bytes 3244040 | tf_op jit(solution)/shard_map/ppermute | solution.py:90
  30.1 27.5 %copy-start.12 = (bf16[128,4224]{1,0:T(8,128)(2,1)}, bf16[128,4224]{1,0:T(8,128)(2,1)S(1)}, u32[]{:S(2)}) copy-start(bf16[128,4224]{1,0:T(8,128)(2,1)S(1)} %collective-permute-done.1) | copy-start | bytes 3244036
  30.2 25.0 %collective-permute-start.2 = (bf16[128,4224]{1,0:T(8,128)(2,1)S(1)}, bf16[128,4224]{1,0:T(8,128)(2,1)S(1)}, u32[]{:S(2)}, u32[]{:S(2)}) collective-permute-start(bf16[128,4224]{1,0:T(8,128)(2,1)S(1)} %collective-permute-done.1), channel_id=1, source_target_pairs={{0,4},{1,5},{4,8},{5,9},{8,12},{9,13},{12,14},{13,15},{14,10},{15,... | collective-permute-start | bytes 3244040 | tf_op jit(solution)/shard_map/ppermute | solution.py:87
  32.0 24.7 %copy-start.10 = (bf16[128,4224]{1,0:T(8,128)(2,1)}, bf16[128,4224]{1,0:T(8,128)(2,1)S(1)}, u32[]{:S(2)}) copy-start(bf16[128,4224]{1,0:T(8,128)(2,1)S(1)} %collective-permute-done.3) | copy-start | bytes 3244036
  32.0 24.7 %collective-permute-start.4 = (bf16[128,4224]{1,0:T(8,128)(2,1)S(1)}, bf16[128,4224]{1,0:T(8,128)(2,1)S(1)}, u32[]{:S(2)}, u32[]{:S(2)}) collective-permute-start(bf16[128,4224]{1,0:T(8,128)(2,1)S(1)} %collective-permute-done.3), channel_id=1, source_target_pairs={{4,0},{5,1},{8,4},{9,5},{12,8},{13,9},{14,12},{15,13},{10,14},{11,... | collective-permute-start | bytes 3244040 | tf_op jit(solution)/shard_map/ppermute | solution.py:90
  55.2 1.5 copy-start.6
  55.2 24.1 %collective-permute-start.6 = (bf16[128,4224]{1,0:T(8,128)(2,1)S(1)}, bf16[128,4224]{1,0:T(8,128)(2,1)S(1)}, u32[]{:S(2)}, u32[]{:S(2)}) collective-permute-start(bf16[128,4224]{1,0:T(8,128)(2,1)S(1)} %collective-permute-done.2), channel_id=1, source_target_pairs={{0,4},{1,5},{4,8},{5,9},{8,12},{9,13},{12,14},{13,15},{14,10},{15,... | collective-permute-start | bytes 3244040 | tf_op jit(solution)/shard_map/ppermute | solution.py:87
  56.7 36.8 %copy-start.8 = (bf16[128,4224]{1,0:T(8,128)(2,1)}, bf16[128,4224]{1,0:T(8,128)(2,1)S(1)}, u32[]{:S(2)}) copy-start(bf16[128,4224]{1,0:T(8,128)(2,1)S(1)} %collective-permute-done.4) | copy-start | bytes 3244036
  56.7 36.8 %collective-permute-start.7 = (bf16[128,4224]{1,0:T(8,128)(2,1)S(1)}, bf16[128,4224]{1,0:T(8,128)(2,1)S(1)}, u32[]{:S(2)}, u32[]{:S(2)}) collective-permute-start(bf16[128,4224]{1,0:T(8,128)(2,1)S(1)} %collective-permute-done.4), channel_id=1, source_target_pairs={{4,0},{5,1},{8,4},{9,5},{12,8},{13,9},{14,12},{15,13},{10,14},{11,... | collective-permute-start | bytes 3244040 | tf_op jit(solution)/shard_map/ppermute | solution.py:90
  79.3 1.0 copy-start.4
  81.2 13.5 %collective-permute-start.9 = (bf16[64,4224]{1,0:T(8,128)(2,1)}, bf16[64,4224]{1,0:T(8,128)(2,1)}, u32[]{:S(2)}, u32[]{:S(2)}) collective-permute-start(bf16[64,4224]{1,0:T(8,128)(2,1)} %slice.94), channel_id=1, source_target_pairs={{0,4},{1,5},{4,8},{5,9},{8,12},{9,13},{12,14},{13,15},{14,10},{15,... | collective-permute-start | bytes 1622024 | tf_op jit(solution)/shard_map/ppermute | solution.py:87
  93.5 11.5 %copy-start.13 = (bf16[128,4224]{1,0:T(8,128)(2,1)S(1)}, bf16[128,4224]{1,0:T(8,128)(2,1)}, u32[]{:S(2)}) copy-start(bf16[128,4224]{1,0:T(8,128)(2,1)} %copy-done.12) | copy-start | bytes 3244036
  93.5 1.2 copy-start.2
  93.6 12.5 %copy-start.5 = (bf16[128,4224]{1,0:T(8,128)(2,1)S(1)}, bf16[128,4224]{1,0:T(8,128)(2,1)}, u32[]{:S(2)}) copy-start(bf16[128,4224]{1,0:T(8,128)(2,1)} %copy-done.4) | copy-start | bytes 3244036
  93.6 11.3 %collective-permute-start.10 = (bf16[64,4224]{1,0:T(8,128)(2,1)S(1)}, bf16[64,4224]{1,0:T(8,128)(2,1)S(1)}, u32[]{:S(2)}, u32[]{:S(2)}) collective-permute-start(bf16[64,4224]{1,0:T(8,128)(2,1)S(1)} %slice.95), channel_id=1, source_target_pairs={{4,0},{5,1},{8,4},{9,5},{12,8},{13,9},{14,12},{15,13},{10,14},{11,... | collective-permute-start | bytes 1622024 | tf_op jit(solution)/shard_map/ppermute | solution.py:90
  104.9 2.8 collective-permute-start.11
  108.0 18.4 %copy-start.3 = (bf16[128,4224]{1,0:T(8,128)(2,1)S(1)}, bf16[128,4224]{1,0:T(8,128)(2,1)}, u32[]{:S(2)}) copy-start(bf16[128,4224]{1,0:T(8,128)(2,1)} %copy-done.2) | copy-start | bytes 3244036
  108.0 18.4 %copy-start.18 = (bf16[256,4224]{1,0:T(8,128)(2,1)S(1)}, bf16[256,4224]{1,0:T(8,128)(2,1)}, u32[]{:S(2)}) copy-start(bf16[256,4224]{1,0:T(8,128)(2,1)} %constant_dynamic-update-slice_fusion.3) | copy-start | bytes 6488068
  108.0 19.0 %copy-start.16 = (bf16[256,4224]{1,0:T(8,128)(2,1)S(1)}, bf16[256,4224]{1,0:T(8,128)(2,1)}, u32[]{:S(2)}) copy-start(bf16[256,4224]{1,0:T(8,128)(2,1)} %constant_dynamic-update-slice_fusion.7) | copy-start | bytes 6488068
  126.2 1.2 copy-start.11
  126.2 2.7 collective-permute-start.12
  126.5 8.6 %copy-start.19 = (bf16[256,4224]{1,0:T(8,128)(2,1)}, bf16[256,4224]{1,0:T(8,128)(2,1)S(1)}, u32[]{:S(2)}) copy-start(bf16[256,4224]{1,0:T(8,128)(2,1)S(1)} %constant_dynamic-update-slice_fusion.2.a_ref) | copy-start | bytes 6488068
  126.5 5.5 %collective-permute-start.8 = (bf16[256,4224]{1,0:T(8,128)(2,1)S(1)}, bf16[256,4224]{1,0:T(8,128)(2,1)S(1)}, u32[]{:S(2)}, u32[]{:S(2)}) collective-permute-start(bf16[256,4224]{1,0:T(8,128)(2,1)S(1)} %constant_dynamic-update-slice_fusion.2.a_ref), channel_id=1, source_target_pairs={{0,1},{1,0},{2,3},{3,2},{4,5},{5,4},{6,7},{7,6},{8,9},{9,8},{10,11... | collective-permute-start | bytes 6488072 | tf_op jit(solution)/shard_map/ppermute | solution.py:93
  127.5 7.6 %copy-start.17 = (bf16[256,4224]{1,0:T(8,128)(2,1)}, bf16[256,4224]{1,0:T(8,128)(2,1)S(1)}, u32[]{:S(2)}) copy-start(bf16[256,4224]{1,0:T(8,128)(2,1)S(1)} %constant_dynamic-update-slice_fusion.6.a_ref) | copy-start | bytes 6488068
  127.5 7.5 %collective-permute-start.20 = (bf16[256,4224]{1,0:T(8,128)(2,1)S(1)}, bf16[256,4224]{1,0:T(8,128)(2,1)S(1)}, u32[]{:S(2)}, u32[]{:S(2)}) collective-permute-start(bf16[256,4224]{1,0:T(8,128)(2,1)S(1)} %constant_dynamic-update-slice_fusion.6.a_ref), channel_id=1, source_target_pairs={{0,1},{1,0},{2,3},{3,2},{4,5},{5,4},{6,7},{7,6},{8,9},{9,8},{10,11... | collective-permute-start | bytes 6488072 | tf_op jit(solution)/shard_map/ppermute | solution.py:93
  132.0 3.3 %copy-start.24 = (bf16[256,4224]{1,0:T(8,128)(2,1)}, bf16[256,4224]{1,0:T(8,128)(2,1)S(1)}, u32[]{:S(2)}) copy-start(bf16[256,4224]{1,0:T(8,128)(2,1)S(1)} %collective-permute-done.8.b_ref) | copy-start | bytes 6488068
  135.1 1.3 copy-start.23
  136.7 25.9 %copy-start.7 = (bf16[128,4224]{1,0:T(8,128)(2,1)S(1)}, bf16[128,4224]{1,0:T(8,128)(2,1)}, u32[]{:S(2)}) copy-start(bf16[128,4224]{1,0:T(8,128)(2,1)} %copy-done.6) | copy-start | bytes 3244036
  162.3 1.2 copy-start.9
  162.4 4.2 %collective-permute-start.13 = (bf16[256,4096]{1,0:T(8,128)(2,1)S(1)}, bf16[256,4096]{1,0:T(8,128)(2,1)S(1)}, u32[]{:S(2)}, u32[]{:S(2)}) collective-permute-start(bf16[256,4096]{1,0:T(8,128)(2,1)S(1)} %get-tuple-element.32), channel_id=1, source_target_pairs={{0,1},{1,0},{2,3},{3,2},{4,5},{5,4},{6,7},{7,6},{8,9},{9,8},{10,11... | collective-permute-start | bytes 6291464 | tf_op jit(solution)/shard_map/ppermute | solution.py:93
  163.7 17.5 %copy-start.20 = (bf16[256,4224]{1,0:T(8,128)(2,1)}, bf16[256,4224]{1,0:T(8,128)(2,1)S(1)}, u32[]{:S(2)}) copy-start(bf16[256,4224]{1,0:T(8,128)(2,1)S(1)} %constant_dynamic-update-slice_fusion.a_ref) | copy-start | bytes 6488068
  163.7 17.5 %collective-permute-start.5 = (bf16[256,4224]{1,0:T(8,128)(2,1)S(1)}, bf16[256,4224]{1,0:T(8,128)(2,1)S(1)}, u32[]{:S(2)}, u32[]{:S(2)}) collective-permute-start(bf16[256,4224]{1,0:T(8,128)(2,1)S(1)} %constant_dynamic-update-slice_fusion.a_ref), channel_id=1, source_target_pairs={{0,1},{1,0},{2,3},{3,2},{4,5},{5,4},{6,7},{7,6},{8,9},{9,8},{10,11... | collective-permute-start | bytes 6488072 | tf_op jit(solution)/shard_map/ppermute | solution.py:93
  163.9 14.2 %collective-permute-start.14 = (bf16[64,4096]{1,0:T(8,128)(2,1)S(1)}, bf16[64,4096]{1,0:T(8,128)(2,1)S(1)}, u32[]{:S(2)}, u32[]{:S(2)}) collective-permute-start(bf16[64,4096]{1,0:T(8,128)(2,1)S(1)} %get-tuple-element.33), channel_id=1, source_target_pairs={{0,4},{1,5},{4,8},{5,9},{8,12},{9,13},{12,14},{13,15},{14,10},{15,... | collective-permute-start | bytes 1572872 | tf_op jit(solution)/shard_map/ppermute | solution.py:87
  165.5 13.9 %collective-permute-start.15 = (bf16[64,4096]{1,0:T(8,128)(2,1)S(1)}, bf16[64,4096]{1,0:T(8,128)(2,1)S(1)}, u32[]{:S(2)}, u32[]{:S(2)}) collective-permute-start(bf16[64,4096]{1,0:T(8,128)(2,1)S(1)} %get-tuple-element.34), channel_id=1, source_target_pairs={{4,0},{5,1},{8,4},{9,5},{12,8},{13,9},{14,12},{15,13},{10,14},{11,... | collective-permute-start | bytes 1572872 | tf_op jit(solution)/shard_map/ppermute | solution.py:90
  181.2 1.3 copy-start.22
  210.1 28.6 %collective-permute-start.16 = (bf16[256,4096]{1,0:T(8,128)(2,1)}, bf16[256,4096]{1,0:T(8,128)(2,1)}, u32[]{:S(2)}, u32[]{:S(2)}) collective-permute-start(bf16[256,4096]{1,0:T(8,128)(2,1)} %get-tuple-element.38), channel_id=1, source_target_pairs={{0,1},{1,0},{2,3},{3,2},{4,5},{5,4},{6,7},{7,6},{8,9},{9,8},{10,11... | collective-permute-start | bytes 6291464 | tf_op jit(solution)/shard_map/ppermute | solution.py:93
  210.3 26.3 %copy-start.15 = (bf16[128,4096]{1,0:T(8,128)(2,1)S(1)}, bf16[128,4096]{1,0:T(8,128)(2,1)}, u32[]{:S(2)}) copy-start(bf16[128,4096]{1,0:T(8,128)(2,1)} %get-tuple-element.39) | copy-start | bytes 3145732
  210.4 27.9 %copy-start.14 = (bf16[128,4096]{1,0:T(8,128)(2,1)S(1)}, bf16[128,4096]{1,0:T(8,128)(2,1)}, u32[]{:S(2)}) copy-start(bf16[128,4096]{1,0:T(8,128)(2,1)} %get-tuple-element.40) | copy-start | bytes 3145732
  236.0 31.6 %collective-permute-start.21 = (bf16[256,4096]{1,0:T(8,128)(2,1)S(1)}, bf16[256,4096]{1,0:T(8,128)(2,1)S(1)}, u32[]{:S(2)}, u32[]{:S(2)}) collective-permute-start(bf16[256,4096]{1,0:T(8,128)(2,1)S(1)} %get-tuple-element.46), channel_id=1, source_target_pairs={{0,1},{1,0},{2,3},{3,2},{4,5},{5,4},{6,7},{7,6},{8,9},{9,8},{10,11... | collective-permute-start | bytes 6291464 | tf_op jit(solution)/shard_map/ppermute | solution.py:93
  236.6 29.0 %collective-permute-start = (bf16[128,4224]{1,0:T(8,128)(2,1)S(1)}, bf16[128,4224]{1,0:T(8,128)(2,1)S(1)}, u32[]{:S(2)}, u32[]{:S(2)}) collective-permute-start(bf16[128,4224]{1,0:T(8,128)(2,1)S(1)} %pad_maximum_fusion.a_ref), channel_id=1, source_target_pairs={{0,1},{1,0},{2,3},{3,2},{4,5},{5,4},{6,7},{7,6},{8,9},{9,8},{10,11... | collective-permute-start | bytes 3244040 | tf_op jit(solution)/shard_map/ppermute | solution.py:93
  236.7 25.5 %collective-permute-start.17 = (bf16[128,4096]{1,0:T(8,128)(2,1)S(1)}, bf16[128,4096]{1,0:T(8,128)(2,1)S(1)}, u32[]{:S(2)}, u32[]{:S(2)}) collective-permute-start(bf16[128,4096]{1,0:T(8,128)(2,1)S(1)} %copy-done.15), channel_id=1, source_target_pairs={{0,4},{1,5},{4,8},{5,9},{8,12},{9,13},{12,14},{13,15},{14,10},{15,... | collective-permute-start | bytes 3145736 | tf_op jit(solution)/shard_map/ppermute | solution.py:87
  238.2 25.2 %collective-permute-start.18 = (bf16[128,4096]{1,0:T(8,128)(2,1)S(1)}, bf16[128,4096]{1,0:T(8,128)(2,1)S(1)}, u32[]{:S(2)}, u32[]{:S(2)}) collective-permute-start(bf16[128,4096]{1,0:T(8,128)(2,1)S(1)} %copy-done.14), channel_id=1, source_target_pairs={{4,0},{5,1},{8,4},{9,5},{12,8},{13,9},{14,12},{15,13},{10,14},{11,... | collective-permute-start | bytes 3145736 | tf_op jit(solution)/shard_map/ppermute | solution.py:90
  265.6 2.8 copy-start
  265.6 24.7 %collective-permute-start.22 = (bf16[128,4096]{1,0:T(8,128)(2,1)}, bf16[128,4096]{1,0:T(8,128)(2,1)}, u32[]{:S(2)}, u32[]{:S(2)}) collective-permute-start(bf16[128,4096]{1,0:T(8,128)(2,1)} %get-tuple-element.47), channel_id=1, source_target_pairs={{0,4},{1,5},{4,8},{5,9},{8,12},{9,13},{12,14},{13,15},{14,10},{15,... | collective-permute-start | bytes 3145736 | tf_op jit(solution)/shard_map/ppermute | solution.py:87
  267.1 24.4 %collective-permute-start.24 = (bf16[128,4096]{1,0:T(8,128)(2,1)}, bf16[128,4096]{1,0:T(8,128)(2,1)}, u32[]{:S(2)}, u32[]{:S(2)}) collective-permute-start(bf16[128,4096]{1,0:T(8,128)(2,1)} %get-tuple-element.48), channel_id=1, source_target_pairs={{4,0},{5,1},{8,4},{9,5},{12,8},{13,9},{14,12},{15,13},{10,14},{11,... | collective-permute-start | bytes 3145736 | tf_op jit(solution)/shard_map/ppermute | solution.py:90
  268.7 1.2 copy-start.1
  288.0 7.9 %collective-permute-start.19 = (bf16[128,4096]{1,0:T(8,128)(2,1)S(1)}, bf16[128,4096]{1,0:T(8,128)(2,1)S(1)}, u32[]{:S(2)}, u32[]{:S(2)}) collective-permute-start(bf16[128,4096]{1,0:T(8,128)(2,1)S(1)} %get-tuple-element.44), channel_id=1, source_target_pairs={{0,1},{1,0},{2,3},{3,2},{4,5},{5,4},{6,7},{7,6},{8,9},{9,8},{10,11... | collective-permute-start | bytes 3145736 | tf_op jit(solution)/shard_map/ppermute | solution.py:93
  293.9 23.3 %collective-permute-start.23 = (bf16[128,4096]{1,0:T(8,128)(2,1)S(1)}, bf16[128,4096]{1,0:T(8,128)(2,1)S(1)}, u32[]{:S(2)}, u32[]{:S(2)}) collective-permute-start(bf16[128,4096]{1,0:T(8,128)(2,1)S(1)} %get-tuple-element.59), channel_id=1, source_target_pairs={{0,4},{1,5},{4,8},{5,9},{8,12},{9,13},{12,14},{13,15},{14,10},{15,... | collective-permute-start | bytes 3145736 | tf_op jit(solution)/shard_map/ppermute | solution.py:87
  294.6 23.1 %collective-permute-start.25 = (bf16[128,4096]{1,0:T(8,128)(2,1)S(1)}, bf16[128,4096]{1,0:T(8,128)(2,1)S(1)}, u32[]{:S(2)}, u32[]{:S(2)}) collective-permute-start(bf16[128,4096]{1,0:T(8,128)(2,1)S(1)} %get-tuple-element.60), channel_id=1, source_target_pairs={{4,0},{5,1},{8,4},{9,5},{12,8},{13,9},{14,12},{15,13},{10,14},{11,... | collective-permute-start | bytes 3145736 | tf_op jit(solution)/shard_map/ppermute | solution.py:90
